TPU v7x, 128 devices: a whole 4x4x4 slice. The times are simulated.
128 devices in a mesh: wide: 16 (over y, z_lo, core), narrow: 8 (over z_hi, x).
Axes of the slice: x: 4, y: 4, z: 4 (z_hi: 2, z_lo: 2; z = z_hi * 2 + z_lo), core: 2. Of those that a mesh axis runs over, the one named last changes fastest.
Arguments:
- gradient: bfloat16 [3584, 18432], P(('wide', 'narrow')), may hold values from -3000 to 3000
Outputs:
- update: bfloat16 [3584, 18432], P(('wide', 'narrow'))
All inputs are finite; a program needn't handle non-finite values.
Results may differ from a plain program's by a relative error of at most 0.0055.
Values may be sent and summed in bfloat16 or wider, within the bound.
A program may use at most 64 MiB of HBM per device.

v0:
```python
import math

import jax
import jax.numpy as jnp
from jax import lax
from jax.experimental import pallas as pl
from jax.experimental.pallas import tpu as pltpu
from jax.sharding import PartitionSpec as P

M = 3584
K = 18432

COEFF_A = 3.4445
COEFF_B = -4.775
COEFF_C = 2.0315

MESH = pl.DeviceIdType.MESH
BF = jnp.bfloat16
F32 = jnp.float32
NT = (((1,), (1,)), ((), ()))

ROWS = 28
PIECE = 32
THIRD = K // 3
COL1 = THIRD // 4
COL2 = COL1 // 4
COL3 = COL2 // 4
CHIP = 3 * COL3
HALF_M = M // 2
AXES = ((0, 1, 2), (1, 2, 0), (2, 0, 1))

BLK = 256
NB = M // BLK
PER_PART = (10, 8)
SECOND = 3 * PER_PART[0]
SLOTS = 3 * sum(PER_PART)
SIZES = ((1280, 320, 80), (1024, 256, 64))


def al(x, m=16):
    return pl.multiple_of(x, m)


def kernel(
    in_ref, y0,
    rows_in, x0, x2, x2p, x3, s_all, st,
    ut, y2p, y2,
    ta, tb, g, r1a, r2a, r3a, r1b, r2b, r3b, sq, yf, ybf, yp, yr, zf, zp, zr,
    io_sem, in_send, in_recv, in_plane_send, in_plane_recv, core_send, core_recv,
    out_send, out_recv, out_plane_send, out_plane_recv, part_send, part_recv,
    rsa_send, rsa_recv, aga_send, aga_recv, rsb_send, rsb_recv, agb_send, agb_recv, sq_send, sq_recv,
):
    w, n_ = lax.axis_index("wide"), lax.axis_index("narrow")
    core, z_lo, y = w % 2, (w // 2) % 2, w // 4
    x, z_hi = n_ % 4, n_ // 4
    z = z_hi * 2 + z_lo
    pos = (x, y, z)

    def device(x, y, z, core):
        return ((y * 2 + z % 2) * 2 + core, (z // 2) * 4 + x)

    def shifted(axis, by):
        p = [x, y, z]
        p[axis] = (p[axis] + by) % 4
        return device(*p, core)

    right = [shifted(a, 1) for a in range(3)]
    left = [shifted(a, 3) for a in range(3)]
    across = [shifted(a, 2) for a in range(3)]
    partner = device(x, y, z, 1 - core)

    def in_plane(p, d, e):
        a, b, _ = AXES[p]
        if e == 0:
            return (right, across, left)[d - 1][a]
        if d == 0:
            return (right, across, left)[e - 1][b]
        v = [x, y, z]
        v[a] = (v[a] + d) % 4
        v[b] = (v[b] + e) % 4
        return device(*v, core)

    steps = [(d, e) for d in range(4) for e in range(4) if d or e]
    plane_devices = [[in_plane(p, d, e) for d, e in steps] for p in range(3)]
    diagonal = [plane_devices[p][k] for p in range(3) for k, (d, e) in enumerate(steps) if d and e]

    barrier = pltpu.get_barrier_semaphore()
    for d in right + left + across + diagonal + [partner]:
        pl.semaphore_signal(barrier, inc=1, device_id=d, device_id_type=MESH)

    fetch = pltpu.make_async_copy(in_ref, rows_in, io_sem.at[0])
    fetch.start()
    fetch.wait()

    def load(k, carry):
        p, q = k // 4, k % 4
        v = rows_in[:, pl.ds(al(k * COL1, COL1), COL1)]
        for e in range(4):
            x0[p, q * 4 + e, pl.ds(0, ROWS), :] = v[:, e * COL2 : (e + 1) * COL2]
            x0[p, q * 4 + e, pl.ds(ROWS, PIECE - ROWS), :] = jnp.zeros((PIECE - ROWS, COL2), BF)
        return carry

    lax.fori_loop(0, 12, load, 0)
    pl.semaphore_wait(barrier, 37)

    def remote(src, dst, send, recv, dev):
        return pltpu.make_async_remote_copy(
            src_ref=src, dst_ref=dst, send_sem=send, recv_sem=recv, device_id=dev, device_id_type=MESH
        )

    sent = []

    def flush(group):
        for c in group:
            c.wait_send()
        group.clear()

    class Exchange:
        def __init__(self, stage, axis_no, src, dst, sems):
            self.stage, self.axis_no, self.src, self.dst, self.sems = stage, axis_no, src, dst, sems
            self.copies = {}

        def begin(self, p):
            a = AXES[p][self.axis_no]
            me = pos[a]
            send, recv = self.sems
            group = []
            for k, dev in ((2, across[a]), (1, right[a]), (3, left[a])):
                c = remote(
                    self.src(p, (me + k) % 4), self.dst(p, me),
                    send.at[self.stage, p, k - 1], recv.at[self.stage, p, k - 1], dev,
                )
                c.start()
                group.append(c)
                sent.append(c)
            self.copies[p] = group

        def keep(self, p):
            me = pos[AXES[p][self.axis_no]]
            src, dst = self.src(p, me), self.dst(p, me)
            dst[...] = src[...]

        def arrive(self, p):
            for c in self.copies[p]:
                c.wait_recv()

    def spot(p, a, b):
        return b * 4 + a if p == 2 else a * 4 + b

    class PlaneExchange:
        def __init__(self, src, dst, src_spot, dst_spot, send, recv):
            self.src, self.dst, self.src_spot, self.dst_spot = src, dst, src_spot, dst_spot
            self.send, self.recv = send, recv

        def begin(self, p):
            a, b, _ = AXES[p]
            here = self.dst(p, self.dst_spot(p, pos[a], pos[b]))
            for (d, e), dev in zip(steps, plane_devices[p]):
                there = self.src_spot(p, (pos[a] + d) % 4, (pos[b] + e) % 4)
                remote(self.src.at[p, there], here, self.send.at[p], self.recv.at[p], dev).start()

        def keep(self, p):
            a, b, _ = AXES[p]
            self.dst(p, self.dst_spot(p, pos[a], pos[b]))[...] = self.src[p, self.src_spot(p, pos[a], pos[b])]

        def arrive(self, p):
            all_of = self.src.at[p, pl.ds(0, 15)]
            pltpu.make_async_copy(all_of, all_of, self.recv.at[p]).wait()

        def left(self, p):
            all_of = self.src.at[p, pl.ds(0, 15)]
            pltpu.make_async_copy(all_of, all_of, self.send.at[p]).wait()

    ins = (in_send, in_recv)
    outs = (out_send, out_recv)
    columns = lambda p, a, b: a * 4 + b
    in1 = PlaneExchange(x0, lambda p, s: x2.at[p, s], columns, spot, in_plane_send, in_plane_recv)
    in3 = Exchange(0, 2, lambda p, q: x2p.at[p, q], lambda p, q: x3.at[core, p, q], ins)
    for p in range(3):
        in1.begin(p)

    def square(k, total):
        for e in range(4):
            v = x0[k // 4, k % 4 * 4 + e].astype(F32)
            v = v * v
            v = (v[:, :128] + v[:, 128:256]) + v[:, 256:]
            total = total + ((v[:8] + v[8:16]) + (v[16:24] + v[24:]))
        return total

    for p in range(3):
        in1.keep(p)
    sq[13] = lax.fori_loop(0, 12, square, jnp.zeros((8, 128), F32))
    sq_core = remote(sq.at[13], sq.at[14], sq_send.at[3, 0], sq_recv.at[3, 0], partner)
    sq_core.start()
    sent.append(sq_core)

    def iota(shape, d):
        return lax.broadcasted_iota(jnp.int32, shape, d)

    def ones_where(cond):
        return jnp.where(cond, 1.0, 0.0).astype(BF)

    def spread_matrix(shape, wide, unit, narrow):
        s, r = iota(shape, wide), iota(shape, 1 - wide)
        return ones_where((s % unit < narrow) & (r == (s // unit) * narrow + s % unit))

    widen = spread_matrix((COL2, 512), 1, 128, COL3)
    for p in range(3):
        in1.arrive(p)
        for u in range(4):
            rows = x2[p, pl.ds(4 * u, 4)].reshape(4 * PIECE, COL2)
            rows = jnp.dot(rows, widen, preferred_element_type=F32).astype(BF)
            for q in range(4):
                x2p[p, q, u] = rows[:, q * 128 : (q + 1) * 128].reshape(4, PIECE, 128)
        in3.begin(p)
    for p in range(3):
        in3.keep(p)
    crossing = []
    for p in range(3):
        in3.arrive(p)
        here = x3.at[core, p]
        c = remote(here, here, core_send.at[p], core_recv.at[p], partner)
        c.start()
        crossing.append(c)
        sent.append(c)

    pack = spread_matrix((8 * ROWS, 8 * PIECE), 1, PIECE, ROWS)

    def pack_rows(owner):
        def body(k, carry):
            x, y0, group = k // 2, k % 2 * 2, [[], [], []]
            for y in (y0, y0 + 1):
                for z in range(4):
                    group[0].append(x3[owner, 0, z, x, y])
                    group[1].append(x3[owner, 1, x, y, z])
                    group[2].append(x3[owner, 2, y, x, z])
            rows = jnp.concatenate([jnp.concatenate(e, axis=0) for e in group], axis=1)
            at = pl.ds(al(owner * HALF_M + k * 8 * ROWS), 8 * ROWS)
            s_all[at, :] = jnp.dot(pack, rows, preferred_element_type=F32).astype(BF)
            return carry

        lax.fori_loop(0, 4, lambda k, carry: body(2 * k + 1, body(2 * k, carry)), 0)

    pack_rows(core)
    for c in crossing:
        c.wait_recv()
    pack_rows(1 - core)

    def turn_all():
        kk, ll = iota((CHIP, 384), 0), iota((CHIP, 384), 1)
        pick = ones_where((ll % 128 < COL3) & (kk == (ll // 128) * COL3 + ll % 128))

        def turn(j, carry):
            at = pl.ds(al(j * BLK, BLK), BLK)
            st[:, at] = lax.dot_general(pick, s_all[at, :], NT, preferred_element_type=F32).astype(BF)
            return carry

        lax.fori_loop(0, NB // 2, lambda k, carry: turn(2 * k + 1, turn(2 * k, carry)), 0)

    def block_of(chunk, m):
        if chunk == 0:
            i = jnp.where(m < 28, m % NB, 4 * core + m - 28)
            d = jnp.where(m < 28, 2 * core + m // NB, 7)
            return i, d, jnp.where(d == 0, 0.5, 1.0)
        i = jnp.where(m < 14, m, jnp.where(m < 21, 7 * core + m - 14, (4 * core + m - 19) % NB))
        d = jnp.where(m < 14, 4 + 2 * core, jnp.where(m < 21, 5, 7))
        return i, d, jnp.where((d == 7) & ((i >= 7) | (m == 23)), 0.0, 1.0)

    def gram_block(chunk, m, t):
        i, d, scale = block_of(chunk, m)
        j = (i + d) % NB
        ri = pl.ds(al(i * BLK, BLK), BLK)
        rj = pl.ds(al(j * BLK, BLK), BLK)
        acc = lax.dot_general(s_all[ri, :], s_all[rj, :], NT, preferred_element_type=F32)
        acc = (scale * acc).astype(BF)
        t[pl.ds(al(m * 512, 512), 256), :] = acc[:, :128]
        t[pl.ds(al(m * 512 + 256, 256), 256), :] = acc[:, 128:]

    def square_begin(s):
        group = [
            remote(sq.at[4 * s], sq.at[4 * s + 1 + k], sq_send.at[s, k], sq_recv.at[s, k], dev)
            for k, dev in enumerate((right[s], left[s], across[s]))
        ]
        for c in group:
            c.start()
        sent.extend(group)
        return group

    def square_end(s, group):
        for c in group:
            c.wait_recv()
        sq[4 * s + 4] = (sq[4 * s] + sq[4 * s + 3]) + (sq[4 * s + 1] + sq[4 * s + 2])

    class Chunk:
        def __init__(self, no, t, bufs, rs, ag):
            self.no, self.t, self.bufs, self.rs, self.ag = no, t, bufs, rs, ag
            self.blocks = PER_PART[no]
            self.sizes = SIZES[no]
            base = [p * self.blocks * 512 for p in range(3)]
            self.bases = [base]
            for k in range(3):
                base = [base[p] + pos[AXES[p][k]] * self.sizes[k] for p in range(3)]
                self.bases.append(base)
            self.mine = no * SECOND * 512
            self.copies = {}

        def quarter(self, k, p, by):
            return self.bases[k][p] + ((pos[AXES[p][k]] + by) % 4) * self.sizes[k]

        def gram(self, p, start, count):
            for m in range(count):
                gram_block(self.no, p * self.blocks + start + m, self.t)

        def gram_far(self):
            for p in range(3):
                q = (pos[AXES[p][0]] + 2) % 4
                self.gram(p, self.blocks * q // 4, 2 + self.blocks % 4 // 2)

        def gram_near(self):
            for p in range(3):
                me = pos[AXES[p][0]]
                if self.blocks % 4:
                    self.gram(p, self.blocks // 4 + self.blocks // 2 * (me // 2), 1)
                for by in (1, 3):
                    self.gram(p, (self.blocks * ((me + by) % 4) + 2) // 4, 2)

        def gram_own(self):
            for p in range(3):
                self.gram(p, (self.blocks * pos[AXES[p][0]] + 2) // 4, 2)

        def push(self, k, p, no, off, rows):
            a = AXES[p][k]
            c = remote(
                self.t.at[pl.ds(al(off), rows), :],
                self.bufs[k].at[p, no],
                self.rs[0].at[k, p, no],
                self.rs[1].at[k, p, no],
                right[a] if no < 3 else left[a],
            )
            c.start()
            self.copies[k, p, no] = c
            sent.append(c)

        def add_rows(self, off, rows, srcs):
            step = rows // 2 if rows > 200 else rows
            t = self.t

            def body(m, carry):
                at = pl.ds(al(off + m * step), step)
                total = t[at, :]
                for src in srcs:
                    total = total + src[pl.ds(al(m * step), step), :]
                t[at, :] = total
                return carry

            lax.fori_loop(0, rows // step, body, 0)

        def scatter_far(self, k):
            half = self.sizes[k] // 2
            for p in range(3):
                self.push(k, p, 0, self.quarter(k, p, 2), half)
                self.push(k, p, 3, self.quarter(k, p, 2) + half, half)

        def scatter_near(self, k):
            half = self.sizes[k] // 2
            for p in range(3):
                self.push(k, p, 1, self.quarter(k, p, 1) + half, half)
                self.push(k, p, 4, self.quarter(k, p, 3), half)

        def scatter_mid(self, k):
            half = self.sizes[k] // 2
            for p in range(3):
                self.copies[k, p, 0].wait_recv()
                self.add_rows(self.quarter(k, p, 1), half, [self.bufs[k].at[p, 0]])
                self.push(k, p, 2, self.quarter(k, p, 1), half)
                self.copies[k, p, 3].wait_recv()
                self.add_rows(self.quarter(k, p, 3) + half, half, [self.bufs[k].at[p, 3]])
                self.push(k, p, 5, self.quarter(k, p, 3) + half, half)

        def scatter_end(self, k):
            half = self.sizes[k] // 2
            for p in range(3):
                for h, one, two in ((0, 4, 2), (1, 1, 5)):
                    self.copies[k, p, one].wait_recv()
                    self.copies[k, p, two].wait_recv()
                    self.add_rows(
                        self.quarter(k, p, 0) + h * half, half, [self.bufs[k].at[p, one], self.bufs[k].at[p, two]]
                    )

        def ring_begin(self, s):
            size = self.sizes[s]
            for p in range(3):
                a = AXES[p][s]
                for k, dev in ((2, across[a]), (1, right[a]), (3, left[a])):
                    c = remote(
                        self.t.at[pl.ds(al(self.quarter(s, p, k)), size), :],
                        self.bufs[s].at[p, k - 1],
                        self.rs[0].at[s, p, k - 1],
                        self.rs[1].at[s, p, k - 1],
                        dev,
                    )
                    c.start()
                    self.copies[s, p, k] = c
                    sent.append(c)

        def ring_end(self, s):
            size = self.sizes[s]
            for p in range(3):
                for k in (1, 2, 3):
                    self.copies[s, p, k].wait_recv()
                off = self.bases[s + 1][p]
                step = 80 if size % 80 == 0 else 64

                def body(m, carry):
                    at = pl.ds(al(off + m * step), step)
                    total = self.t[at, :].astype(F32)
                    for k in range(3):
                        total = total + self.bufs[s][p, k, pl.ds(al(m * step), step)].astype(F32)
                    if s == 2:
                        g[pl.ds(al(self.mine + off), size), :] = total.astype(BF)
                    else:
                        self.t[at, :] = total.astype(BF)
                    return carry

                lax.fori_loop(0, size // step, body, 0)
            if s == 2:
                self.rounds(2)

        def rounds(self, s):
            for p in range(3):
                a = AXES[p][s]
                off = self.bases[s + 1][p]
                for k, dev in ((2, across[a]), (1, right[a]), (3, left[a])):
                    self.spread(s, p, k - 1, off, self.sizes[s], dev)

        def rounds_end(self, s):
            for p in range(3):
                self.got(s, p, 0, 1, 2)

        def spread(self, k, p, no, off, rows, dev):
            here = g.at[pl.ds(al(self.mine + off), rows), :]
            c = remote(here, here, self.ag[0].at[k, p, no], self.ag[1].at[k, p, no], dev)
            c.start()
            self.copies["g", k, p, no] = c
            sent.append(c)

        def got(self, k, p, *nos):
            for no in nos:
                self.copies["g", k, p, no].wait_recv()

        def gather_begin(self, k):
            half = self.sizes[k] // 2
            for p in range(3):
                own = self.quarter(k, p, 0)
                a = AXES[p][k]
                self.spread(k, p, 0, own, half, right[a])
                self.spread(k, p, 1, own + half, half, left[a])
            for p in range(3):
                own = self.quarter(k, p, 0)
                a = AXES[p][k]
                self.spread(k, p, 2, own + half, half, right[a])
                self.spread(k, p, 3, own, half, left[a])

        def gather_mid(self, k):
            half = self.sizes[k] // 2
            for p in range(3):
                a = AXES[p][k]
                self.got(k, p, 0)
                self.spread(k, p, 4, self.quarter(k, p, 3), half, right[a])
                self.got(k, p, 1)
                self.spread(k, p, 5, self.quarter(k, p, 1) + half, half, left[a])

        def gather_end(self, k):
            for p in range(3):
                self.got(k, p, 2, 3, 4, 5)

    one = Chunk(0, ta, (r1a, r2a, r3a), (rsa_send, rsa_recv), (aga_send, aga_recv))
    two = Chunk(1, tb, (r1b, r2b, r3b), (rsb_send, rsb_recv), (agb_send, agb_recv))

    early = list(sent)
    sent.clear()
    one.gram_far()
    one.scatter_far(0)
    one.gram_near()
    one.scatter_near(0)
    two.gram_far()
    one.gram_own()
    one.scatter_mid(0)
    two.scatter_far(0)
    two.gram_near()
    two.scatter_near(0)
    two.gram_own()
    sq_core.wait_recv()
    sq[0] = sq[13] + sq[14]
    squares = square_begin(0)
    turn_all()
    flush(early)
    for p in range(3):
        in1.left(p)
    one.scatter_end(0)
    one.ring_begin(1)
    square_end(0, squares)
    squares = square_begin(1)
    two.scatter_mid(0)
    one.ring_end(1)
    one.ring_begin(2)
    square_end(1, squares)
    squares = square_begin(2)
    two.scatter_end(0)
    two.ring_begin(1)
    one.ring_end(2)
    square_end(2, squares)
    two.ring_end(1)
    two.ring_begin(2)
    one.rounds_end(2)
    one.rounds(1)
    two.ring_end(2)
    one.rounds_end(1)
    early.extend(sent)
    sent.clear()
    one.gather_begin(0)
    two.rounds_end(2)
    two.rounds(1)
    one.gather_mid(0)
    two.rounds_end(1)
    two.gather_begin(0)
    flush(early)
    one.gather_end(0)

    def cols(a_ref, i):
        return a_ref[:, pl.ds(al(i * BLK, BLK), BLK)]

    def block(slot):
        o = slot * 512
        return jnp.concatenate([g[pl.ds(al(o, 512), 256), :], g[pl.ds(al(o + 256, 256), 256), :]], axis=1)

    def band(a_ref, j, ds):
        def straight(d, first):
            i = (j + NB - d) % NB
            return cols(a_ref, i), block(first + i)

        def turned(d, first):
            return cols(a_ref, (j + d) % NB), block(first + j)

        a, b = zip(*[straight(*e) for e in ds])
        acc = jnp.dot(jnp.concatenate(a, axis=1), jnp.concatenate(b, axis=0), preferred_element_type=F32)
        a, b = zip(*[turned(*e) for e in ds])
        return acc + lax.dot_general(
            jnp.concatenate(a, axis=1), jnp.concatenate(b, axis=1), NT, preferred_element_type=F32
        )

    whole_one = ((2 * core, 0), (2 * core + 1, NB))
    whole_two = ((2 * core + 4, SECOND),)

    def single(acc_ref, a_ref, chunk, m):
        i, d, _ = block_of(chunk, m)
        j = (i + d) % NB
        b = block(chunk * SECOND + m)
        acc_ref[:, pl.ds(al(j * BLK, BLK), BLK)] += jnp.dot(cols(a_ref, i), b, preferred_element_type=F32)
        acc_ref[:, pl.ds(al(i * BLK, BLK), BLK)] += lax.dot_general(
            cols(a_ref, j), b, NT, preferred_element_type=F32
        )

    def loop(first_k, last_k, f):
        def body(k, carry):
            f(first_k + 2 * k)
            f(first_k + 2 * k + 1)
            return carry

        lax.fori_loop(0, (last_k - first_k) // 2, body, 0)
        if (last_k - first_k) % 2:
            f(last_k - 1)

    def band_at(j):
        return pl.ds(al(j * BLK, BLK), BLK)

    def to_partner(no, src, dst):
        c = remote(src, dst, part_send.at[no], part_recv.at[no], partner)
        c.start()
        sent.append(c)
        return c

    def y_one(j):
        yf[:, band_at(j)] = band(st, j, whole_one)

    loop(0, 6, y_one)
    two.gather_mid(0)
    loop(6, NB, y_one)
    zf[...] = jnp.zeros((CHIP, M), F32)
    for m in (28, 29):
        single(yf, st, 0, m)
    two.gather_end(0)
    def shared(k, a_ref=st, acc_ref=yf):
        single(acc_ref, a_ref, 1, 14 + k)

    loop(0, 9, shared)

    def y_two(j):
        v = yf[:, band_at(j)] + band(st, j, whole_two)
        yf[:, band_at(j)] = v
        yp[:, band_at(j)] = v.astype(BF)

    shares = []
    for h in range(2):
        loop(h * 7, h * 7 + 7, y_two)
        here = pl.ds(h * HALF_M, HALF_M)
        shares.append(to_partner(h, yp.at[:, here], yr.at[:, here]))

    factor = 0.3 * math.sqrt(M) / (jnp.sqrt(jnp.sum(sq[12], axis=(0, 1), keepdims=True)) + 1e-07)
    factor2 = factor * factor

    def y_sum(j):
        v = factor2 * (yf[:, band_at(j)] + yr[:, band_at(j)].astype(F32))
        yf[:, band_at(j)] = v
        ybf[:, band_at(j)] = v.astype(BF)

    for h in range(2):
        shares[h].wait_recv()
        loop(h * 7, h * 7 + 7, y_sum)

    for m in (28, 29):
        single(zf, ybf, 0, m)
    def shared(k, a_ref=ybf, acc_ref=zf):
        single(acc_ref, a_ref, 1, 14 + k)

    loop(0, 9, shared)

    def z_band(j):
        return factor2 * (zf[:, band_at(j)] + band(ybf, j, whole_one + whole_two))

    def z_theirs(k):
        zp[:, band_at(k)] = z_band((1 - core) * 7 + k).astype(BF)

    loop(0, 7, z_theirs)
    share = to_partner(2, zp, zr)

    def z_mine(k):
        zf[:, band_at(core * 7 + k)] = z_band(core * 7 + k)

    loop(0, 7, z_mine)
    share.wait_recv()
    for p in range(3):
        ut[pl.ds(p * 128 + COL3, 128 - COL3), :] = jnp.zeros((128 - COL3, HALF_M), BF)

    def finish(k):
        at = band_at(core * 7 + k)
        scaled = (factor * st[:, at].astype(F32)).astype(BF).astype(F32)
        product = factor * (COEFF_B * yf[:, at] + COEFF_C * (zf[:, at] + zr[:, band_at(k)].astype(F32)))
        u = (math.sqrt(K) * (COEFF_A * scaled + product)).astype(BF)
        for p in range(3):
            ut[pl.ds(p * 128, COL3), band_at(k)] = u[p * COL3 : (p + 1) * COL3]

    loop(0, 7, finish)

    early.extend(sent)
    sent.clear()
    y3 = x2p
    unpack = spread_matrix((8 * PIECE, 8 * ROWS), 0, PIECE, ROWS)
    for m in range(8):
        o = m * 8 * ROWS
        first_lane = o // 128 * 128
        skip = o - first_lane
        width = -(-(skip + 8 * ROWS) // 128) * 128
        v = ut[:, pl.ds(first_lane, width)][:, skip : skip + 8 * ROWS]
        rows = lax.dot_general(unpack, v, NT, preferred_element_type=F32).astype(BF)
        for r in range(8):
            x, y, z = m // 2, m % 2 * 2 + r // 4, r % 4
            for p, at in enumerate(((z, x, y), (x, y, z), (y, x, z))):
                y3[(p,) + at] = rows[r * PIECE : (r + 1) * PIECE, p * 128 : (p + 1) * 128]

    out1 = Exchange(0, 2, lambda p, q: y3.at[p, q], lambda p, q: y2p.at[p, q], outs)
    out2 = PlaneExchange(
        y2, lambda p, s: y0.at[:, pl.ds(al(p * THIRD + s * COL2, 128), COL2)], spot, columns, out_plane_send, out_plane_recv,
    )
    for p in range(3):
        out1.begin(p)
    for p in range(3):
        out1.keep(p)
    flush(early)
    early.extend(sent)
    sent.clear()
    narrow = spread_matrix((512, COL2), 0, 128, COL3)
    for p in range(3):
        out1.arrive(p)
        for u in range(4):
            rows = [y2p[p, q, u].reshape(4 * PIECE, 128) for q in range(4)]
            rows = jnp.dot(jnp.concatenate(rows, axis=1), narrow, preferred_element_type=F32)
            y2[p, pl.ds(4 * u, 4)] = rows.astype(BF).reshape(4, PIECE, COL2)
        out2.begin(p)
    own = []
    for p in range(3):
        a, b, _ = AXES[p]
        at = (pos[a], pos[b])
        own.append(pltpu.make_async_copy(y2.at[p, spot(p, *at)], out2.dst(p, columns(p, *at)), io_sem.at[1 + p]))
        own[p].start()
    flush(early)
    for p in range(3):
        out2.arrive(p)
        own[p].wait()
    for p in range(3):
        out2.left(p)
    flush(sent)


def local(gradient):
    dma = pltpu.SemaphoreType.DMA
    hbm = pl.BlockSpec(memory_space=pl.ANY)
    padded = pl.pallas_call(
        kernel,
        out_shape=jax.ShapeDtypeStruct((PIECE, K), BF),
        in_specs=[hbm],
        out_specs=hbm,
        scratch_shapes=[
            pltpu.VMEM((ROWS, K), BF),
            pltpu.VMEM((3, 16, PIECE, COL2), BF),
            pltpu.VMEM((3, 16, PIECE, COL2), BF),
            pltpu.VMEM((3, 4, 4, 4, PIECE, 128), BF),
            pltpu.VMEM((2, 3, 4, 4, 4, PIECE, 128), BF),
            pltpu.VMEM((M, 384), BF),
            pltpu.VMEM((CHIP, M), BF),
            pltpu.VMEM((384, HALF_M), BF),
            pltpu.VMEM((3, 4, 4, 4, PIECE, 128), BF),
            pltpu.VMEM((3, 16, PIECE, COL2), BF),
            pltpu.VMEM((3 * 10 * 512, 128), BF),
            pltpu.VMEM((3 * 8 * 512, 128), BF),
            pltpu.VMEM((SLOTS * 512, 128), BF),
            pltpu.VMEM((3, 6, 640, 128), BF),
            pltpu.VMEM((3, 3, 320, 128), BF),
            pltpu.VMEM((3, 3, 80, 128), BF),
            pltpu.VMEM((3, 6, 512, 128), BF),
            pltpu.VMEM((3, 3, 256, 128), BF),
            pltpu.VMEM((3, 3, 64, 128), BF),
            pltpu.VMEM((15, 8, 128), F32),
            pltpu.VMEM((CHIP, M), F32),
            pltpu.VMEM((CHIP, M), BF),
            pltpu.VMEM((CHIP, M), BF),
            pltpu.VMEM((CHIP, M), BF),
            pltpu.VMEM((CHIP, M), F32),
            pltpu.VMEM((CHIP, HALF_M), BF),
            pltpu.VMEM((CHIP, HALF_M), BF),
            dma((4,)),
            dma((1, 3, 3)),
            dma((1, 3, 3)),
            dma((3,)),
            dma((3,)),
            dma((3,)),
            dma((3,)),
            dma((1, 3, 3)),
            dma((1, 3, 3)),
            dma((3,)),
            dma((3,)),
            dma((3,)),
            dma((3,)),
            dma((3, 3, 6)),
            dma((3, 3, 6)),
            dma((3, 3, 6)),
            dma((3, 3, 6)),
            dma((3, 3, 6)),
            dma((3, 3, 6)),
            dma((3, 3, 6)),
            dma((3, 3, 6)),
            dma((4, 3)),
            dma((4, 3)),
        ],
        compiler_params=pltpu.CompilerParams(
            collective_id=0, has_side_effects=True, vmem_limit_bytes=60 * 1024 * 1024
        ),
        cost_estimate=pl.CostEstimate(flops=16 * 10**9, bytes_accessed=5 * 10**6, transcendentals=0),
    )(gradient)
    return padded[:ROWS]


def solution(mesh):
    spec = P(("wide", "narrow"), None)
    return jax.shard_map(local, mesh=mesh, in_specs=(spec,), out_specs=spec, check_vma=False)
```

profile of v0, /device:TPU:1, one launch (start us, length us, event | category | flops | bytes accessed | tf_op | source)
XLA Modules:
  0.0 142.7 jit_solution(3965774768951115263)
XLA Ops:
  0.0 140.4 %shard_map.17 = bf16[32,18432]{1,0:T(8,128)(2,1)} custom-call(bf16[28,18432]{1,0:T(8,128)(2,1)} %in_ref.1), custom_call_target="tpu_custom_call" | custom-call | flops 16000000000 | bytes 5000000 | tf_op jit(solution)/shard_map/pallas_call | solution.py:708
  140.4 2.4 %copy.3 = bf16[28,18432]{1,0:T(8,128)(2,1)} copy(bf16[28,18432]{1,0:T(8,128)(2,1)} %bitcast.1) | data formatting | bytes 2064384
where the time goes:
time: 143 us
  Pallas kernels  140 us (98%)
  local copies, waits for them, and re-layouts  2.36 us (2%)
    pallas_call x1, Pallas kernels, local(): pl.pallas_call(kernel, out_shape=jax.ShapeDtypeStruct((PIECE, K), BF), in...  140 us

commit v1 on v0

--- a/solution.py
+++ b/solution.py
@@ -31,10 +31,10 @@
 
 BLK = 256
 NB = M // BLK
-PER_PART = (10, 8)
+PER_PART = (12, 6)
 SECOND = 3 * PER_PART[0]
 SLOTS = 3 * sum(PER_PART)
-SIZES = ((1280, 320, 80), (1024, 256, 64))
+SIZES = ((1536, 384, 96), (768, 192, 48))
 
 
 def al(x, m=16):
@@ -259,12 +259,12 @@
 
     def block_of(chunk, m):
         if chunk == 0:
-            i = jnp.where(m < 28, m % NB, 4 * core + m - 28)
-            d = jnp.where(m < 28, 2 * core + m // NB, 7)
+            i = jnp.where(m < 28, m % NB, jnp.where(m < 35, 7 * core + m - 28, 4 * core))
+            d = jnp.where(m < 28, 2 * core + m // NB, jnp.where(m < 35, 5, 7))
             return i, d, jnp.where(d == 0, 0.5, 1.0)
-        i = jnp.where(m < 14, m, jnp.where(m < 21, 7 * core + m - 14, (4 * core + m - 19) % NB))
-        d = jnp.where(m < 14, 4 + 2 * core, jnp.where(m < 21, 5, 7))
-        return i, d, jnp.where((d == 7) & ((i >= 7) | (m == 23)), 0.0, 1.0)
+        i = jnp.where(m < 14, m, 4 * core + jnp.minimum(m, 16) - 13)
+        d = jnp.where(m < 14, 4 + 2 * core, 7)
+        return i, d, jnp.where((d == 7) & ((i >= 7) | (m == 17)), 0.0, 1.0)
 
     def gram_block(chunk, m, t):
         i, d, scale = block_of(chunk, m)
@@ -314,7 +314,7 @@
         def gram_far(self):
             for p in range(3):
                 q = (pos[AXES[p][0]] + 2) % 4
-                self.gram(p, self.blocks * q // 4, 2 + self.blocks % 4 // 2)
+                self.gram(p, self.blocks * q // 4, -(-self.blocks // 4))
 
         def gram_near(self):
             for p in range(3):
@@ -322,11 +322,11 @@
                 if self.blocks % 4:
                     self.gram(p, self.blocks // 4 + self.blocks // 2 * (me // 2), 1)
                 for by in (1, 3):
-                    self.gram(p, (self.blocks * ((me + by) % 4) + 2) // 4, 2)
+                    self.gram(p, (self.blocks * ((me + by) % 4) + 2) // 4, self.blocks // 4)
 
         def gram_own(self):
             for p in range(3):
-                self.gram(p, (self.blocks * pos[AXES[p][0]] + 2) // 4, 2)
+                self.gram(p, (self.blocks * pos[AXES[p][0]] + 2) // 4, self.blocks // 4)
 
         def push(self, k, p, no, off, rows):
             a = AXES[p][k]
@@ -409,7 +409,7 @@
                 for k in (1, 2, 3):
                     self.copies[s, p, k].wait_recv()
                 off = self.bases[s + 1][p]
-                step = 80 if size % 80 == 0 else 64
+                step = min(size, 96)
 
                 def body(m, carry):
                     at = pl.ds(al(off + m * step), step)
@@ -583,17 +583,17 @@
     def y_one(j):
         yf[:, band_at(j)] = band(st, j, whole_one)
 
+    def shared(acc_ref, a_ref):
+        return lambda m: single(acc_ref, a_ref, 0, 28 + m), lambda m: single(acc_ref, a_ref, 1, 14 + m)
+
+    y_first, y_rest = shared(yf, st)
     loop(0, 6, y_one)
     two.gather_mid(0)
     loop(6, NB, y_one)
     zf[...] = jnp.zeros((CHIP, M), F32)
-    for m in (28, 29):
-        single(yf, st, 0, m)
+    loop(0, 8, y_first)
     two.gather_end(0)
-    def shared(k, a_ref=st, acc_ref=yf):
-        single(acc_ref, a_ref, 1, 14 + k)
-
-    loop(0, 9, shared)
+    loop(0, 3, y_rest)
 
     def y_two(j):
         v = yf[:, band_at(j)] + band(st, j, whole_two)
@@ -618,12 +618,9 @@
         shares[h].wait_recv()
         loop(h * 7, h * 7 + 7, y_sum)
 
-    for m in (28, 29):
-        single(zf, ybf, 0, m)
-    def shared(k, a_ref=ybf, acc_ref=zf):
-        single(acc_ref, a_ref, 1, 14 + k)
-
-    loop(0, 9, shared)
+    z_first, z_rest = shared(zf, ybf)
+    loop(0, 8, z_first)
+    loop(0, 3, z_rest)
 
     def z_band(j):
         return factor2 * (zf[:, band_at(j)] + band(ybf, j, whole_one + whole_two))
@@ -721,15 +718,15 @@
             pltpu.VMEM((384, HALF_M), BF),
             pltpu.VMEM((3, 4, 4, 4, PIECE, 128), BF),
             pltpu.VMEM((3, 16, PIECE, COL2), BF),
-            pltpu.VMEM((3 * 10 * 512, 128), BF),
-            pltpu.VMEM((3 * 8 * 512, 128), BF),
+            pltpu.VMEM((3 * 12 * 512, 128), BF),
+            pltpu.VMEM((3 * 6 * 512, 128), BF),
             pltpu.VMEM((SLOTS * 512, 128), BF),
-            pltpu.VMEM((3, 6, 640, 128), BF),
-            pltpu.VMEM((3, 3, 320, 128), BF),
-            pltpu.VMEM((3, 3, 80, 128), BF),
-            pltpu.VMEM((3, 6, 512, 128), BF),
-            pltpu.VMEM((3, 3, 256, 128), BF),
-            pltpu.VMEM((3, 3, 64, 128), BF),
+            pltpu.VMEM((3, 6, 768, 128), BF),
+            pltpu.VMEM((3, 3, 384, 128), BF),
+            pltpu.VMEM((3, 3, 96, 128), BF),
+            pltpu.VMEM((3, 6, 384, 128), BF),
+            pltpu.VMEM((3, 3, 192, 128), BF),
+            pltpu.VMEM((3, 3, 48, 128), BF),
             pltpu.VMEM((15, 8, 128), F32),
             pltpu.VMEM((CHIP, M), F32),
             pltpu.VMEM((CHIP, M), BF),

time: 143 us -> 142 us (level)
  no operation moved by 1% of the time
where the time goes in v1:
time: 142 us
  Pallas kernels  139 us (98%)
  local copies, waits for them, and re-layouts  2.36 us (2%)
    pallas_call x1, Pallas kernels, local(): pl.pallas_call(kernel, out_shape=jax.ShapeDtypeStruct((PIECE, K), BF), in...  139 us

profile of v1, /device:TPU:1, one launch (start us, length us, event | category | flops | bytes accessed | tf_op | source)
XLA Modules:
  0.0 141.6 jit_solution(5749779939533570695)
XLA Ops:
  0.0 139.2 %shard_map.17 = bf16[32,18432]{1,0:T(8,128)(2,1)} custom-call(bf16[28,18432]{1,0:T(8,128)(2,1)} %in_ref.1), custom_call_target="tpu_custom_call" | custom-call | flops 16000000000 | bytes 5000000 | tf_op jit(solution)/shard_map/pallas_call | solution.py:705
  139.2 2.4 %copy.3 = bf16[28,18432]{1,0:T(8,128)(2,1)} copy(bf16[28,18432]{1,0:T(8,128)(2,1)} %bitcast.1) | data formatting | bytes 2064384

commit v2 on v1

--- a/solution.py
+++ b/solution.py
@@ -296,6 +296,7 @@
             self.no, self.t, self.bufs, self.rs, self.ag = no, t, bufs, rs, ag
             self.blocks = PER_PART[no]
             self.sizes = SIZES[no]
+            self.size0 = self.sizes[0]
             base = [p * self.blocks * 512 for p in range(3)]
             self.bases = [base]
             for k in range(3):
@@ -461,6 +462,25 @@
                 self.spread(k, p, 2, own + half, half, right[a])
                 self.spread(k, p, 3, own, half, left[a])
 
+        def piece(self, i):
+            rows = self.size0 // 4
+            for p in range(3):
+                own = self.quarter(0, p, 0)
+                self.spread(0, p, i, own + i * rows, rows, right[p])
+                self.spread(0, p, 4 + i, own + (i + 2) % 4 * rows, rows, left[p])
+
+        def hand_on(self, i):
+            rows = self.size0 // 4
+            for p in range(3):
+                self.got(0, p, i)
+                self.spread(0, p, 8 + i, self.quarter(0, p, 3) + i * rows, rows, right[p])
+                self.got(0, p, 4 + i)
+                self.spread(0, p, 10 + i, self.quarter(0, p, 1) + (i + 2) * rows, rows, left[p])
+
+        def pieces_end(self):
+            for p in range(3):
+                self.got(0, p, 2, 3, 6, 7, 8, 9, 10, 11)
+
         def gather_mid(self, k):
             half = self.sizes[k] // 2
             for p in range(3):
@@ -488,7 +508,6 @@
     one.scatter_mid(0)
     two.scatter_far(0)
     two.gram_near()
-    two.scatter_near(0)
     two.gram_own()
     sq_core.wait_recv()
     sq[0] = sq[13] + sq[14]
@@ -499,33 +518,38 @@
         in1.left(p)
     one.scatter_end(0)
     one.ring_begin(1)
+    two.scatter_near(0)
     square_end(0, squares)
     squares = square_begin(1)
-    two.scatter_mid(0)
     one.ring_end(1)
     one.ring_begin(2)
+    two.scatter_mid(0)
     square_end(1, squares)
     squares = square_begin(2)
+    one.ring_end(2)
     two.scatter_end(0)
     two.ring_begin(1)
-    one.ring_end(2)
     square_end(2, squares)
+    one.rounds_end(2)
+    one.rounds(1)
     two.ring_end(1)
     two.ring_begin(2)
-    one.rounds_end(2)
-    one.rounds(1)
-    two.ring_end(2)
     one.rounds_end(1)
     early.extend(sent)
     sent.clear()
-    one.gather_begin(0)
+    one.piece(0)
+    two.ring_end(2)
+    one.piece(1)
     two.rounds_end(2)
     two.rounds(1)
-    one.gather_mid(0)
+    one.piece(2)
+    one.hand_on(0)
     two.rounds_end(1)
+    one.piece(3)
+    one.hand_on(1)
     two.gather_begin(0)
     flush(early)
-    one.gather_end(0)
+    one.pieces_end()
 
     def cols(a_ref, i):
         return a_ref[:, pl.ds(al(i * BLK, BLK), BLK)]
@@ -750,8 +774,8 @@
             dma((3,)),
             dma((3, 3, 6)),
             dma((3, 3, 6)),
-            dma((3, 3, 6)),
-            dma((3, 3, 6)),
+            dma((3, 3, 12)),
+            dma((3, 3, 12)),
             dma((3, 3, 6)),
             dma((3, 3, 6)),
             dma((3, 3, 6)),

time: 142 us -> 142 us (level)
  no operation moved by 1% of the time
where the time goes in v2:
time: 142 us
  Pallas kernels  140 us (99%)
  local copies, waits for them, and re-layouts  2.36 us (2%)
    pallas_call x1, Pallas kernels, local(): pl.pallas_call(kernel, out_shape=jax.ShapeDtypeStruct((PIECE, K), BF), in...  140 us

profile of v2, /device:TPU:1, one launch (start us, length us, event | category | flops | bytes accessed | tf_op | source)
XLA Modules:
  0.0 142.0 jit_solution(3105285194060179978)
XLA Ops:
  0.0 139.7 %shard_map.17 = bf16[32,18432]{1,0:T(8,128)(2,1)} custom-call(bf16[28,18432]{1,0:T(8,128)(2,1)} %in_ref.1), custom_call_target="tpu_custom_call" | custom-call | flops 16000000000 | bytes 5000000 | tf_op jit(solution)/shard_map/pallas_call | solution.py:729
  139.7 2.4 %copy.3 = bf16[28,18432]{1,0:T(8,128)(2,1)} copy(bf16[28,18432]{1,0:T(8,128)(2,1)} %bitcast.1) | data formatting | bytes 2064384

commit v3 on v1

--- a/solution.py
+++ b/solution.py
@@ -152,12 +152,16 @@
             self.src, self.dst, self.src_spot, self.dst_spot = src, dst, src_spot, dst_spot
             self.send, self.recv = send, recv
 
+        def start(self, p, k):
+            a, b, _ = AXES[p]
+            d, e = steps[k]
+            here = self.dst(p, self.dst_spot(p, pos[a], pos[b]))
+            there = self.src_spot(p, (pos[a] + d) % 4, (pos[b] + e) % 4)
+            remote(self.src.at[p, there], here, self.send.at[p], self.recv.at[p], plane_devices[p][k]).start()
+
         def begin(self, p):
-            a, b, _ = AXES[p]
-            here = self.dst(p, self.dst_spot(p, pos[a], pos[b]))
-            for (d, e), dev in zip(steps, plane_devices[p]):
-                there = self.src_spot(p, (pos[a] + d) % 4, (pos[b] + e) % 4)
-                remote(self.src.at[p, there], here, self.send.at[p], self.recv.at[p], dev).start()
+            for k in range(15):
+                self.start(p, k)
 
         def keep(self, p):
             a, b, _ = AXES[p]
@@ -176,8 +180,9 @@
     columns = lambda p, a, b: a * 4 + b
     in1 = PlaneExchange(x0, lambda p, s: x2.at[p, s], columns, spot, in_plane_send, in_plane_recv)
     in3 = Exchange(0, 2, lambda p, q: x2p.at[p, q], lambda p, q: x3.at[core, p, q], ins)
-    for p in range(3):
-        in1.begin(p)
+    for k in range(15):
+        for p in range(3):
+            in1.start(p, k)
 
     def square(k, total):
         for e in range(4):
@@ -389,15 +394,14 @@
 
         def ring_begin(self, s):
             size = self.sizes[s]
-            for p in range(3):
-                a = AXES[p][s]
-                for k, dev in ((2, across[a]), (1, right[a]), (3, left[a])):
+            for k, dev in ((2, across), (1, right), (3, left)):
+                for p in range(3):
                     c = remote(
                         self.t.at[pl.ds(al(self.quarter(s, p, k)), size), :],
                         self.bufs[s].at[p, k - 1],
                         self.rs[0].at[s, p, k - 1],
                         self.rs[1].at[s, p, k - 1],
-                        dev,
+                        dev[AXES[p][s]],
                     )
                     c.start()
                     self.copies[s, p, k] = c
@@ -427,11 +431,9 @@
                 self.rounds(2)
 
         def rounds(self, s):
-            for p in range(3):
-                a = AXES[p][s]
-                off = self.bases[s + 1][p]
-                for k, dev in ((2, across[a]), (1, right[a]), (3, left[a])):
-                    self.spread(s, p, k - 1, off, self.sizes[s], dev)
+            for k, dev in ((2, across), (1, right), (3, left)):
+                for p in range(3):
+                    self.spread(s, p, k - 1, self.bases[s + 1][p], self.sizes[s], dev[AXES[p][s]])
 
         def rounds_end(self, s):
             for p in range(3):
@@ -601,10 +603,10 @@
         yp[:, band_at(j)] = v.astype(BF)
 
     shares = []
-    for h in range(2):
-        loop(h * 7, h * 7 + 7, y_two)
-        here = pl.ds(h * HALF_M, HALF_M)
-        shares.append(to_partner(h, yp.at[:, here], yr.at[:, here]))
+    for lo, hi in ((0, 4), (4, 8), (8, 12), (12, 14)):
+        loop(lo, hi, y_two)
+        here = pl.ds(lo * BLK, (hi - lo) * BLK)
+        shares.append((lo, hi, to_partner(len(shares), yp.at[:, here], yr.at[:, here])))
 
     factor = 0.3 * math.sqrt(M) / (jnp.sqrt(jnp.sum(sq[12], axis=(0, 1), keepdims=True)) + 1e-07)
     factor2 = factor * factor
@@ -614,9 +616,9 @@
         yf[:, band_at(j)] = v
         ybf[:, band_at(j)] = v.astype(BF)
 
-    for h in range(2):
-        shares[h].wait_recv()
-        loop(h * 7, h * 7 + 7, y_sum)
+    for lo, hi, arriving in shares:
+        arriving.wait_recv()
+        loop(lo, hi, y_sum)
 
     z_first, z_rest = shared(zf, ybf)
     loop(0, 8, z_first)
@@ -629,7 +631,7 @@
         zp[:, band_at(k)] = z_band((1 - core) * 7 + k).astype(BF)
 
     loop(0, 7, z_theirs)
-    share = to_partner(2, zp, zr)
+    share = to_partner(4, zp, zr)
 
     def z_mine(k):
         zf[:, band_at(core * 7 + k)] = z_band(core * 7 + k)
@@ -746,8 +748,8 @@
             dma((1, 3, 3)),
             dma((3,)),
             dma((3,)),
-            dma((3,)),
-            dma((3,)),
+            dma((5,)),
+            dma((5,)),
             dma((3, 3, 6)),
             dma((3, 3, 6)),
             dma((3, 3, 6)),

time: 142 us -> 139 us (0.979)
  Pallas kernels: 139 us -> 137 us
    pallas_call x1, Pallas kernels: 139 us -> 137 us  [local(): pl.pallas_call(kernel, out_shape=jax.ShapeDtypeStruct((PIECE, K), BF), in...]
where the time goes in v3:
time: 139 us
  Pallas kernels  137 us (99%)
  local copies, waits for them, and re-layouts  2.36 us (2%)
    pallas_call x1, Pallas kernels, local(): pl.pallas_call(kernel, out_shape=jax.ShapeDtypeStruct((PIECE, K), BF), in...  137 us

profile of v3, /device:TPU:1, one launch (start us, length us, event | category | flops | bytes accessed | tf_op | source)
XLA Modules:
  0.0 139.0 jit_solution(7051737091194670113)
XLA Ops:
  0.0 136.7 %shard_map.17 = bf16[32,18432]{1,0:T(8,128)(2,1)} custom-call(bf16[28,18432]{1,0:T(8,128)(2,1)} %in_ref.1), custom_call_target="tpu_custom_call" | custom-call | flops 16000000000 | bytes 5000000 | tf_op jit(solution)/shard_map/pallas_call | solution.py:707
  136.7 2.4 %copy.3 = bf16[28,18432]{1,0:T(8,128)(2,1)} copy(bf16[28,18432]{1,0:T(8,128)(2,1)} %bitcast.1) | data formatting | bytes 2064384

commit v4 on v3

--- a/solution.py
+++ b/solution.py
@@ -108,6 +108,9 @@
             src_ref=src, dst_ref=dst, send_sem=send, recv_sem=recv, device_id=dev, device_id_type=MESH
         )
 
+    def wait_bytes(ref, sem):
+        pltpu.make_async_copy(ref, ref, sem).wait()
+
     sent = []
 
     def flush(group):
@@ -116,24 +119,15 @@
         group.clear()
 
     class Exchange:
-        def __init__(self, stage, axis_no, src, dst, sems):
-            self.stage, self.axis_no, self.src, self.dst, self.sems = stage, axis_no, src, dst, sems
-            self.copies = {}
+        def __init__(self, axis_no, src, dst, sems):
+            self.axis_no, self.src, self.dst = axis_no, src, dst
+            self.send, self.recv = sems
 
         def begin(self, p):
             a = AXES[p][self.axis_no]
             me = pos[a]
-            send, recv = self.sems
-            group = []
             for k, dev in ((2, across[a]), (1, right[a]), (3, left[a])):
-                c = remote(
-                    self.src(p, (me + k) % 4), self.dst(p, me),
-                    send.at[self.stage, p, k - 1], recv.at[self.stage, p, k - 1], dev,
-                )
-                c.start()
-                group.append(c)
-                sent.append(c)
-            self.copies[p] = group
+                remote(self.src(p, (me + k) % 4), self.dst(p, me), self.send.at[p], self.recv.at[p], dev).start()
 
         def keep(self, p):
             me = pos[AXES[p][self.axis_no]]
@@ -141,8 +135,10 @@
             dst[...] = src[...]
 
         def arrive(self, p):
-            for c in self.copies[p]:
-                c.wait_recv()
+            wait_bytes(self.src(p, pl.ds(0, 3)), self.recv.at[p])
+
+        def left(self, p):
+            wait_bytes(self.src(p, pl.ds(0, 3)), self.send.at[p])
 
     def spot(p, a, b):
         return b * 4 + a if p == 2 else a * 4 + b
@@ -168,18 +164,16 @@
             self.dst(p, self.dst_spot(p, pos[a], pos[b]))[...] = self.src[p, self.src_spot(p, pos[a], pos[b])]
 
         def arrive(self, p):
-            all_of = self.src.at[p, pl.ds(0, 15)]
-            pltpu.make_async_copy(all_of, all_of, self.recv.at[p]).wait()
+            wait_bytes(self.src.at[p, pl.ds(0, 15)], self.recv.at[p])
 
         def left(self, p):
-            all_of = self.src.at[p, pl.ds(0, 15)]
-            pltpu.make_async_copy(all_of, all_of, self.send.at[p]).wait()
+            wait_bytes(self.src.at[p, pl.ds(0, 15)], self.send.at[p])
 
     ins = (in_send, in_recv)
     outs = (out_send, out_recv)
     columns = lambda p, a, b: a * 4 + b
     in1 = PlaneExchange(x0, lambda p, s: x2.at[p, s], columns, spot, in_plane_send, in_plane_recv)
-    in3 = Exchange(0, 2, lambda p, q: x2p.at[p, q], lambda p, q: x3.at[core, p, q], ins)
+    in3 = Exchange(2, lambda p, q: x2p.at[p, q], lambda p, q: x3.at[core, p, q], ins)
     for k in range(15):
         for p in range(3):
             in1.start(p, k)
@@ -338,13 +332,12 @@
             c = remote(
                 self.t.at[pl.ds(al(off), rows), :],
                 self.bufs[k].at[p, no],
-                self.rs[0].at[k, p, no],
+                self.rs[0].at[k],
                 self.rs[1].at[k, p, no],
                 right[a] if no < 3 else left[a],
             )
             c.start()
             self.copies[k, p, no] = c
-            sent.append(c)
 
         def add_rows(self, off, rows, srcs):
             step = rows // 2 if rows > 200 else rows
@@ -396,22 +389,18 @@
             size = self.sizes[s]
             for k, dev in ((2, across), (1, right), (3, left)):
                 for p in range(3):
-                    c = remote(
+                    remote(
                         self.t.at[pl.ds(al(self.quarter(s, p, k)), size), :],
                         self.bufs[s].at[p, k - 1],
-                        self.rs[0].at[s, p, k - 1],
-                        self.rs[1].at[s, p, k - 1],
+                        self.rs[0].at[s],
+                        self.rs[1].at[s, p, 0],
                         dev[AXES[p][s]],
-                    )
-                    c.start()
-                    self.copies[s, p, k] = c
-                    sent.append(c)
+                    ).start()
 
         def ring_end(self, s):
             size = self.sizes[s]
             for p in range(3):
-                for k in (1, 2, 3):
-                    self.copies[s, p, k].wait_recv()
+                wait_bytes(self.t.at[pl.ds(0, 3 * size), :], self.rs[1].at[s, p, 0])
                 off = self.bases[s + 1][p]
                 step = min(size, 96)
 
@@ -433,18 +422,22 @@
         def rounds(self, s):
             for k, dev in ((2, across), (1, right), (3, left)):
                 for p in range(3):
-                    self.spread(s, p, k - 1, self.bases[s + 1][p], self.sizes[s], dev[AXES[p][s]])
+                    self.spread(s, p, 0, self.bases[s + 1][p], self.sizes[s], dev[AXES[p][s]])
 
         def rounds_end(self, s):
             for p in range(3):
-                self.got(s, p, 0, 1, 2)
+                wait_bytes(self.t.at[pl.ds(0, 3 * self.sizes[s]), :], self.ag[1].at[s, p, 0])
+
+        def all_sent(self):
+            for s in range(3):
+                for sems in (self.rs, self.ag):
+                    wait_bytes(self.t.at[pl.ds(0, 9 * self.sizes[s]), :], sems[0].at[s])
 
         def spread(self, k, p, no, off, rows, dev):
             here = g.at[pl.ds(al(self.mine + off), rows), :]
-            c = remote(here, here, self.ag[0].at[k, p, no], self.ag[1].at[k, p, no], dev)
+            c = remote(here, here, self.ag[0].at[k], self.ag[1].at[k, p, no], dev)
             c.start()
             self.copies["g", k, p, no] = c
-            sent.append(c)
 
         def got(self, k, p, *nos):
             for no in nos:
@@ -479,8 +472,6 @@
     one = Chunk(0, ta, (r1a, r2a, r3a), (rsa_send, rsa_recv), (aga_send, aga_recv))
     two = Chunk(1, tb, (r1b, r2b, r3b), (rsb_send, rsb_recv), (agb_send, agb_recv))
 
-    early = list(sent)
-    sent.clear()
     one.gram_far()
     one.scatter_far(0)
     one.gram_near()
@@ -496,9 +487,9 @@
     sq[0] = sq[13] + sq[14]
     squares = square_begin(0)
     turn_all()
-    flush(early)
     for p in range(3):
         in1.left(p)
+        in3.left(p)
     one.scatter_end(0)
     one.ring_begin(1)
     square_end(0, squares)
@@ -518,15 +509,12 @@
     one.rounds(1)
     two.ring_end(2)
     one.rounds_end(1)
-    early.extend(sent)
-    sent.clear()
     one.gather_begin(0)
     two.rounds_end(2)
     two.rounds(1)
     one.gather_mid(0)
     two.rounds_end(1)
     two.gather_begin(0)
-    flush(early)
     one.gather_end(0)
 
     def cols(a_ref, i):
@@ -651,8 +639,6 @@
 
     loop(0, 7, finish)
 
-    early.extend(sent)
-    sent.clear()
     y3 = x2p
     unpack = spread_matrix((8 * PIECE, 8 * ROWS), 0, PIECE, ROWS)
     for m in range(8):
@@ -667,7 +653,7 @@
             for p, at in enumerate(((z, x, y), (x, y, z), (y, x, z))):
                 y3[(p,) + at] = rows[r * PIECE : (r + 1) * PIECE, p * 128 : (p + 1) * 128]
 
-    out1 = Exchange(0, 2, lambda p, q: y3.at[p, q], lambda p, q: y2p.at[p, q], outs)
+    out1 = Exchange(2, lambda p, q: y3.at[p, q], lambda p, q: y2p.at[p, q], outs)
     out2 = PlaneExchange(
         y2, lambda p, s: y0.at[:, pl.ds(al(p * THIRD + s * COL2, 128), COL2)], spot, columns, out_plane_send, out_plane_recv,
     )
@@ -675,9 +661,9 @@
         out1.begin(p)
     for p in range(3):
         out1.keep(p)
-    flush(early)
-    early.extend(sent)
-    sent.clear()
+    flush(sent)
+    one.all_sent()
+    two.all_sent()
     narrow = spread_matrix((512, COL2), 0, 128, COL3)
     for p in range(3):
         out1.arrive(p)
@@ -692,13 +678,12 @@
         at = (pos[a], pos[b])
         own.append(pltpu.make_async_copy(y2.at[p, spot(p, *at)], out2.dst(p, columns(p, *at)), io_sem.at[1 + p]))
         own[p].start()
-    flush(early)
+        out1.left(p)
     for p in range(3):
         out2.arrive(p)
         own[p].wait()
     for p in range(3):
         out2.left(p)
-    flush(sent)
 
 
 def local(gradient):
@@ -738,25 +723,25 @@
             pltpu.VMEM((CHIP, HALF_M), BF),
             pltpu.VMEM((CHIP, HALF_M), BF),
             dma((4,)),
-            dma((1, 3, 3)),
-            dma((1, 3, 3)),
-            dma((3,)),
-            dma((3,)),
-            dma((3,)),
-            dma((3,)),
-            dma((1, 3, 3)),
-            dma((1, 3, 3)),
+            dma((3,)),
+            dma((3,)),
+            dma((3,)),
+            dma((3,)),
+            dma((3,)),
+            dma((3,)),
+            dma((3,)),
+            dma((3,)),
             dma((3,)),
             dma((3,)),
             dma((5,)),
             dma((5,)),
+            dma((3,)),
             dma((3, 3, 6)),
+            dma((3,)),
             dma((3, 3, 6)),
+            dma((3,)),
             dma((3, 3, 6)),
-            dma((3, 3, 6)),
-            dma((3, 3, 6)),
-            dma((3, 3, 6)),
-            dma((3, 3, 6)),
+            dma((3,)),
             dma((3, 3, 6)),
             dma((4, 3)),
             dma((4, 3)),

time: 139 us -> 137 us (0.986)
  Pallas kernels: 137 us -> 135 us
    pallas_call x1, Pallas kernels: 137 us -> 135 us  [local(): pl.pallas_call(kernel, out_shape=jax.ShapeDtypeStruct((PIECE, K), BF), in...]
where the time goes in v4:
time: 137 us
  Pallas kernels  135 us (99%)
  local copies, waits for them, and re-layouts  2.36 us (2%)
    pallas_call x1, Pallas kernels, local(): pl.pallas_call(kernel, out_shape=jax.ShapeDtypeStruct((PIECE, K), BF), in...  135 us

profile of v4, /device:TPU:1, one launch (start us, length us, event | category | flops | bytes accessed | tf_op | source)
XLA Modules:
  0.0 137.0 jit_solution(8558891883922675290)
XLA Ops:
  0.0 134.7 %shard_map.17 = bf16[32,18432]{1,0:T(8,128)(2,1)} custom-call(bf16[28,18432]{1,0:T(8,128)(2,1)} %in_ref.1), custom_call_target="tpu_custom_call" | custom-call | flops 16000000000 | bytes 5000000 | tf_op jit(solution)/shard_map/pallas_call | solution.py:692
  134.7 2.4 %copy.3 = bf16[28,18432]{1,0:T(8,128)(2,1)} copy(bf16[28,18432]{1,0:T(8,128)(2,1)} %bitcast.1) | data formatting | bytes 2064384

commit v5 on v4

--- a/solution.py
+++ b/solution.py
@@ -123,11 +123,14 @@
             self.axis_no, self.src, self.dst = axis_no, src, dst
             self.send, self.recv = sems
 
+        def start(self, p, k):
+            a = AXES[p][self.axis_no]
+            dev = (right, across, left)[k - 1][a]
+            remote(self.src(p, (pos[a] + k) % 4), self.dst(p, pos[a]), self.send.at[p], self.recv.at[p], dev).start()
+
         def begin(self, p):
-            a = AXES[p][self.axis_no]
-            me = pos[a]
-            for k, dev in ((2, across[a]), (1, right[a]), (3, left[a])):
-                remote(self.src(p, (me + k) % 4), self.dst(p, me), self.send.at[p], self.recv.at[p], dev).start()
+            for k in (2, 1, 3):
+                self.start(p, k)
 
         def keep(self, p):
             me = pos[AXES[p][self.axis_no]]
@@ -189,9 +192,8 @@
     for p in range(3):
         in1.keep(p)
     sq[13] = lax.fori_loop(0, 12, square, jnp.zeros((8, 128), F32))
-    sq_core = remote(sq.at[13], sq.at[14], sq_send.at[3, 0], sq_recv.at[3, 0], partner)
+    sq_core = remote(sq.at[13], sq.at[14], sq_send.at[0], sq_recv.at[3], partner)
     sq_core.start()
-    sent.append(sq_core)
 
     def iota(shape, d):
         return lax.broadcasted_iota(jnp.int32, shape, d)
@@ -276,18 +278,11 @@
         t[pl.ds(al(m * 512 + 256, 256), 256), :] = acc[:, 128:]
 
     def square_begin(s):
-        group = [
-            remote(sq.at[4 * s], sq.at[4 * s + 1 + k], sq_send.at[s, k], sq_recv.at[s, k], dev)
-            for k, dev in enumerate((right[s], left[s], across[s]))
-        ]
-        for c in group:
-            c.start()
-        sent.extend(group)
-        return group
-
-    def square_end(s, group):
-        for c in group:
-            c.wait_recv()
+        for k, dev in enumerate((right[s], left[s], across[s])):
+            remote(sq.at[4 * s], sq.at[4 * s + 1 + k], sq_send.at[0], sq_recv.at[s], dev).start()
+
+    def square_end(s):
+        wait_bytes(sq.at[pl.ds(0, 3)], sq_recv.at[s])
         sq[4 * s + 4] = (sq[4 * s] + sq[4 * s + 3]) + (sq[4 * s + 1] + sq[4 * s + 2])
 
     class Chunk:
@@ -435,7 +430,7 @@
 
         def spread(self, k, p, no, off, rows, dev):
             here = g.at[pl.ds(al(self.mine + off), rows), :]
-            c = remote(here, here, self.ag[0].at[k], self.ag[1].at[k, p, no], dev)
+            c = remote(here, here, self.ag[0].at[k], self.ag[1].at[k, p, min(no, 2)], dev)
             c.start()
             self.copies["g", k, p, no] = c
 
@@ -467,7 +462,7 @@
 
         def gather_end(self, k):
             for p in range(3):
-                self.got(k, p, 2, 3, 4, 5)
+                wait_bytes(self.t.at[pl.ds(0, 2 * self.sizes[k]), :], self.ag[1].at[k, p, 2])
 
     one = Chunk(0, ta, (r1a, r2a, r3a), (rsa_send, rsa_recv), (aga_send, aga_recv))
     two = Chunk(1, tb, (r1b, r2b, r3b), (rsb_send, rsb_recv), (agb_send, agb_recv))
@@ -485,24 +480,24 @@
     two.gram_own()
     sq_core.wait_recv()
     sq[0] = sq[13] + sq[14]
-    squares = square_begin(0)
+    square_begin(0)
     turn_all()
     for p in range(3):
         in1.left(p)
         in3.left(p)
     one.scatter_end(0)
     one.ring_begin(1)
-    square_end(0, squares)
-    squares = square_begin(1)
+    square_end(0)
+    square_begin(1)
     two.scatter_mid(0)
     one.ring_end(1)
     one.ring_begin(2)
-    square_end(1, squares)
-    squares = square_begin(2)
+    square_end(1)
+    square_begin(2)
     two.scatter_end(0)
     two.ring_begin(1)
     one.ring_end(2)
-    square_end(2, squares)
+    square_end(2)
     two.ring_end(1)
     two.ring_begin(2)
     one.rounds_end(2)
@@ -657,11 +652,13 @@
     out2 = PlaneExchange(
         y2, lambda p, s: y0.at[:, pl.ds(al(p * THIRD + s * COL2, 128), COL2)], spot, columns, out_plane_send, out_plane_recv,
     )
-    for p in range(3):
-        out1.begin(p)
+    for k in (2, 1, 3):
+        for p in range(3):
+            out1.start(p, k)
     for p in range(3):
         out1.keep(p)
     flush(sent)
+    wait_bytes(sq.at[pl.ds(0, 10)], sq_send.at[0])
     one.all_sent()
     two.all_sent()
     narrow = spread_matrix((512, COL2), 0, 128, COL3)
@@ -743,8 +740,8 @@
             dma((3, 3, 6)),
             dma((3,)),
             dma((3, 3, 6)),
-            dma((4, 3)),
-            dma((4, 3)),
+            dma((1,)),
+            dma((4,)),
         ],
         compiler_params=pltpu.CompilerParams(
             collective_id=0, has_side_effects=True, vmem_limit_bytes=60 * 1024 * 1024

time: 137 us -> 137 us (level)
  no operation moved by 1% of the time
where the time goes in v5:
time: 137 us
  Pallas kernels  134 us (98%)
  local copies, waits for them, and re-layouts  2.36 us (2%)
    pallas_call x1, Pallas kernels, local(): pl.pallas_call(kernel, out_shape=jax.ShapeDtypeStruct((PIECE, K), BF), in...  134 us

profile of v5, /device:TPU:1, one launch (start us, length us, event | category | flops | bytes accessed | tf_op | source)
XLA Modules:
  0.0 136.9 jit_solution(4409873296274057667)
XLA Ops:
  0.0 134.5 %shard_map.17 = bf16[32,18432]{1,0:T(8,128)(2,1)} custom-call(bf16[28,18432]{1,0:T(8,128)(2,1)} %in_ref.1), custom_call_target="tpu_custom_call" | custom-call | flops 16000000000 | bytes 5000000 | tf_op jit(solution)/shard_map/pallas_call | solution.py:689
  134.5 2.4 %copy.3 = bf16[28,18432]{1,0:T(8,128)(2,1)} copy(bf16[28,18432]{1,0:T(8,128)(2,1)} %bitcast.1) | data formatting | bytes 2064384

commit v6 on v5

--- a/solution.py
+++ b/solution.py
@@ -50,6 +50,8 @@
     out_send, out_recv, out_plane_send, out_plane_recv, part_send, part_recv,
     rsa_send, rsa_recv, aga_send, aga_recv, rsb_send, rsb_recv, agb_send, agb_recv, sq_send, sq_recv,
 ):
+    fetch = pltpu.make_async_copy(in_ref, rows_in, io_sem.at[0])
+    fetch.start()
     w, n_ = lax.axis_index("wide"), lax.axis_index("narrow")
     core, z_lo, y = w % 2, (w // 2) % 2, w // 4
     x, z_hi = n_ % 4, n_ // 4
@@ -88,8 +90,9 @@
     for d in right + left + across + diagonal + [partner]:
         pl.semaphore_signal(barrier, inc=1, device_id=d, device_id_type=MESH)
 
-    fetch = pltpu.make_async_copy(in_ref, rows_in, io_sem.at[0])
-    fetch.start()
+    for p in range(3):
+        for q in range(16):
+            x0[p, q, pl.ds(ROWS, PIECE - ROWS), :] = jnp.zeros((PIECE - ROWS, COL2), BF)
     fetch.wait()
 
     def load(k, carry):
@@ -97,7 +100,6 @@
         v = rows_in[:, pl.ds(al(k * COL1, COL1), COL1)]
         for e in range(4):
             x0[p, q * 4 + e, pl.ds(0, ROWS), :] = v[:, e * COL2 : (e + 1) * COL2]
-            x0[p, q * 4 + e, pl.ds(ROWS, PIECE - ROWS), :] = jnp.zeros((PIECE - ROWS, COL2), BF)
         return carry
 
     lax.fori_loop(0, 12, load, 0)
@@ -216,6 +218,7 @@
         in3.begin(p)
     for p in range(3):
         in3.keep(p)
+    pack = spread_matrix((8 * ROWS, 8 * PIECE), 1, PIECE, ROWS)
     crossing = []
     for p in range(3):
         in3.arrive(p)
@@ -225,7 +228,6 @@
         crossing.append(c)
         sent.append(c)
 
-    pack = spread_matrix((8 * ROWS, 8 * PIECE), 1, PIECE, ROWS)
 
     def pack_rows(owner):
         def body(k, carry):
@@ -572,9 +574,9 @@
         return lambda m: single(acc_ref, a_ref, 0, 28 + m), lambda m: single(acc_ref, a_ref, 1, 14 + m)
 
     y_first, y_rest = shared(yf, st)
-    loop(0, 6, y_one)
+    loop(0, 4, y_one)
     two.gather_mid(0)
-    loop(6, NB, y_one)
+    loop(4, NB, y_one)
     zf[...] = jnp.zeros((CHIP, M), F32)
     loop(0, 8, y_first)
     two.gather_end(0)

time: 137 us -> 137 us (level)
  no operation moved by 1% of the time
where the time goes in v6:
time: 137 us
  Pallas kernels  135 us (99%)
  local copies, waits for them, and re-layouts  2.36 us (2%)
    pallas_call x1, Pallas kernels, local(): pl.pallas_call(kernel, out_shape=jax.ShapeDtypeStruct((PIECE, K), BF), in...  135 us

profile of v6, /device:TPU:1, one launch (start us, length us, event | category | flops | bytes accessed | tf_op | source)
XLA Modules:
  0.0 137.2 jit_solution(3760396568054382633)
XLA Ops:
  0.0 134.8 %shard_map.17 = bf16[32,18432]{1,0:T(8,128)(2,1)} custom-call(bf16[28,18432]{1,0:T(8,128)(2,1)} %in_ref.1), custom_call_target="tpu_custom_call" | custom-call | flops 16000000000 | bytes 5000000 | tf_op jit(solution)/shard_map/pallas_call | solution.py:691
  134.8 2.4 %copy.3 = bf16[28,18432]{1,0:T(8,128)(2,1)} copy(bf16[28,18432]{1,0:T(8,128)(2,1)} %bitcast.1) | data formatting | bytes 2064384

commit v7 on v6

--- a/solution.py
+++ b/solution.py
@@ -82,7 +82,7 @@
         v[b] = (v[b] + e) % 4
         return device(*v, core)
 
-    steps = [(d, e) for d in range(4) for e in range(4) if d or e]
+    steps = [(d, e) for d in (2, 1, 3, 0) for e in (2, 1, 3, 0) if d or e]
     plane_devices = [[in_plane(p, d, e) for d, e in steps] for p in range(3)]
     diagonal = [plane_devices[p][k] for p in range(3) for k, (d, e) in enumerate(steps) if d and e]
 
@@ -292,6 +292,7 @@
             self.no, self.t, self.bufs, self.rs, self.ag = no, t, bufs, rs, ag
             self.blocks = PER_PART[no]
             self.sizes = SIZES[no]
+            self.size0 = self.sizes[0]
             base = [p * self.blocks * 512 for p in range(3)]
             self.bases = [base]
             for k in range(3):
@@ -307,18 +308,16 @@
             for m in range(count):
                 gram_block(self.no, p * self.blocks + start + m, self.t)
 
-        def gram_far(self):
-            for p in range(3):
-                q = (pos[AXES[p][0]] + 2) % 4
-                self.gram(p, self.blocks * q // 4, -(-self.blocks // 4))
-
-        def gram_near(self):
-            for p in range(3):
-                me = pos[AXES[p][0]]
-                if self.blocks % 4:
-                    self.gram(p, self.blocks // 4 + self.blocks // 2 * (me // 2), 1)
-                for by in (1, 3):
-                    self.gram(p, (self.blocks * ((me + by) % 4) + 2) // 4, self.blocks // 4)
+        def gram_far(self, p):
+            q = (pos[AXES[p][0]] + 2) % 4
+            self.gram(p, self.blocks * q // 4, -(-self.blocks // 4))
+
+        def gram_near(self, p):
+            me = pos[AXES[p][0]]
+            if self.blocks % 4:
+                self.gram(p, self.blocks // 4 + self.blocks // 2 * (me // 2), 1)
+            for by in (1, 3):
+                self.gram(p, (self.blocks * ((me + by) % 4) + 2) // 4, self.blocks // 4)
 
         def gram_own(self):
             for p in range(3):
@@ -350,17 +349,15 @@
 
             lax.fori_loop(0, rows // step, body, 0)
 
-        def scatter_far(self, k):
-            half = self.sizes[k] // 2
-            for p in range(3):
-                self.push(k, p, 0, self.quarter(k, p, 2), half)
-                self.push(k, p, 3, self.quarter(k, p, 2) + half, half)
-
-        def scatter_near(self, k):
-            half = self.sizes[k] // 2
-            for p in range(3):
-                self.push(k, p, 1, self.quarter(k, p, 1) + half, half)
-                self.push(k, p, 4, self.quarter(k, p, 3), half)
+        def scatter_far(self, p):
+            half = self.size0 // 2
+            self.push(0, p, 0, self.quarter(0, p, 2), half)
+            self.push(0, p, 3, self.quarter(0, p, 2) + half, half)
+
+        def scatter_near(self, p):
+            half = self.size0 // 2
+            self.push(0, p, 1, self.quarter(0, p, 1) + half, half)
+            self.push(0, p, 4, self.quarter(0, p, 3), half)
 
         def scatter_mid(self, k):
             half = self.sizes[k] // 2
@@ -469,16 +466,21 @@
     one = Chunk(0, ta, (r1a, r2a, r3a), (rsa_send, rsa_recv), (aga_send, aga_recv))
     two = Chunk(1, tb, (r1b, r2b, r3b), (rsb_send, rsb_recv), (agb_send, agb_recv))
 
-    one.gram_far()
-    one.scatter_far(0)
-    one.gram_near()
-    one.scatter_near(0)
-    two.gram_far()
+    for p in range(3):
+        one.gram_far(p)
+        one.scatter_far(p)
+    for p in range(3):
+        one.gram_near(p)
+        one.scatter_near(p)
+    for p in range(3):
+        two.gram_far(p)
     one.gram_own()
     one.scatter_mid(0)
-    two.scatter_far(0)
-    two.gram_near()
-    two.scatter_near(0)
+    for p in range(3):
+        two.scatter_far(p)
+    for p in range(3):
+        two.gram_near(p)
+        two.scatter_near(p)
     two.gram_own()
     sq_core.wait_recv()
     sq[0] = sq[13] + sq[14]

time: 137 us -> 136 us (level)
  Pallas kernels: 135 us -> 133 us
where the time goes in v7:
time: 136 us
  Pallas kernels  133 us (98%)
  local copies, waits for them, and re-layouts  2.36 us (2%)
    pallas_call x1, Pallas kernels, local(): pl.pallas_call(kernel, out_shape=jax.ShapeDtypeStruct((PIECE, K), BF), in...  133 us

profile of v7, /device:TPU:1, one launch (start us, length us, event | category | flops | bytes accessed | tf_op | source)
XLA Modules:
  0.0 135.9 jit_solution(7856023184261925727)
XLA Ops:
  0.0 133.5 %shard_map.17 = bf16[32,18432]{1,0:T(8,128)(2,1)} custom-call(bf16[28,18432]{1,0:T(8,128)(2,1)} %in_ref.1), custom_call_target="tpu_custom_call" | custom-call | flops 16000000000 | bytes 5000000 | tf_op jit(solution)/shard_map/pallas_call | solution.py:693
  133.5 2.4 %copy.3 = bf16[28,18432]{1,0:T(8,128)(2,1)} copy(bf16[28,18432]{1,0:T(8,128)(2,1)} %bitcast.1) | data formatting | bytes 2064384
